TPU v7x, 32 devices: a whole 2x2x4 slice. The times are simulated.
32 devices in a mesh: dp: 4 (over y, x), seq: 8 (over z, core).
Axes of the slice: x: 2, y: 2, z: 4, core: 2. Of those that a mesh axis runs over, the one named last changes fastest.
Arguments:
- inputs: bfloat16 [2, 4, 2048, 768], P(None, 'dp', 'seq'), may hold values from -6 to 6
- offsets: int32 [2, 4, 2048], P(None, 'dp', 'seq'), may hold values from 0 to 2045, as said below
- w_query: bfloat16 [768, 768], P(('dp', 'seq')), may hold values from -0.21875 to 0.21875
- w_kv: bfloat16 [768, 128], P(('dp', 'seq')), may hold values from -0.21875 to 0.21875
- w_out: bfloat16 [768, 768], P(('dp', 'seq')), may hold values from -0.875 to 0.875
- w_up: bfloat16 [768, 3072], P(('dp', 'seq')), may hold values from -0.21875 to 0.21875
- w_down: bfloat16 [3072, 768], P(('dp', 'seq')), may hold values from -0.109375 to 0.109375
- b_up: bfloat16 [3072], P(('dp', 'seq')), may hold values from -1.5 to 1.5
- vectors: bfloat16 [7, 768], P(None, ('dp', 'seq')), may hold values from -1.5 to 1.5
- b_kv: bfloat16 [128], replicated, may hold values from -2.5 to 2.5
- cotangent: bfloat16 [2, 4, 2048, 768], P(None, 'dp', 'seq'), may hold values from -6 to 6
Outputs:
- out: bfloat16 [2, 4, 2048, 768], P(None, 'dp', 'seq')
- grad_inputs: float32 [2, 4, 2048, 768], P(None, 'dp', 'seq')
- grad_w_query: float32 [768, 768], P(('dp', 'seq'))
- grad_w_kv: float32 [768, 128], P(('dp', 'seq'))
- grad_w_out: float32 [768, 768], P(('dp', 'seq'))
- grad_w_up: float32 [768, 3072], P(('dp', 'seq'))
- grad_w_down: float32 [3072, 768], P(('dp', 'seq'))
- grad_b_up: float32 [3072], P(('dp', 'seq'))
- grad_vectors: float32 [7, 768], P(None, ('dp', 'seq'))
- grad_b_kv: float32 [128], replicated
Inputs may be any that keep to these rules, and one draw needn't show every extreme that they name: Each sequence holds three documents end to end; offsets count 0, 1, 2, ... within each document; the first and the last document have 1 to 128 positions, and in some sequence of every draw both have exactly one.
All inputs are finite; a program needn't handle non-finite values.
Results may differ from a plain program's by a relative error of at most 0.011.
Values may be sent and summed in bfloat16 or wider, within the bound.
A program may use at most 128 MiB of HBM per device.

v0:
```python
import functools
import math

import jax
import jax.numpy as jnp
from jax import lax
from jax.experimental import pallas as pl
from jax.experimental.pallas import tpu as pltpu
from jax.sharding import PartitionSpec as P

H = 12
HD = 64
ROT = 16


epsilon = 1e-05
root_half = 0.7071067811865476
density_scale = 0.3989422804014327
masked_score = -1e30


def normalize(values):
    average = jnp.mean(values, axis=-1, keepdims=True)
    centered = values - average
    inverse = lax.rsqrt(jnp.mean(centered * centered, axis=-1, keepdims=True) + epsilon)
    return (centered * inverse, inverse)


def norm_back(grad_out, normed, inverse, gain_row):
    scaled = grad_out * gain_row
    first_mean = jnp.mean(scaled, axis=-1, keepdims=True)
    second_mean = jnp.mean(scaled * normed, axis=-1, keepdims=True)
    return inverse * (scaled - first_mean - normed * second_mean)


def rotate(values, cosine, sine_part):
    half_rot = ROT // 2
    first_part = values[..., :half_rot]
    second = values[..., half_rot:ROT]
    return jnp.concatenate(
        [
            first_part * cosine - second * sine_part,
            second * cosine + first_part * sine_part,
            values[..., ROT:],
        ],
        axis=-1,
    )


def gelu_slope(hidden):
    return 0.5 * (1.0 + lax.erf(hidden * root_half)) + hidden * density_scale * jnp.exp(
        -0.5 * hidden * hidden
    )


def tree_add(left_tree, right_tree):
    return tuple((left_item + right_item for left_item, right_item in zip(left_tree, right_tree)))


def plain_on_device(inputs, offsets, w_query, w_kv, w_out, w_up, w_down, b_up, vectors, b_kv, cotangent):
    micro_count = inputs.shape[0]
    local_rows = inputs.shape[2]
    model_width = inputs.shape[3]
    seqlen = local_rows * lax.axis_size("seq")
    key_block = math.gcd(seqlen, 512)
    first_row = lax.axis_index("seq") * local_rows
    blocks_used = (first_row + local_rows + key_block - 1) // key_block
    row_ids = first_row + jnp.arange(local_rows, dtype=jnp.int32)
    half_rot = ROT // 2
    frequency = jnp.power(10000.0, -jnp.arange(half_rot, dtype=jnp.float32) * (2.0 / ROT))
    kv_bias = b_kv.astype(jnp.float32)
    results = []
    input_grads = []
    totals = None
    kv_bias_total = jnp.zeros(b_kv.shape, jnp.float32)
    for micro_index in range(micro_count):
        values_in = inputs[micro_index, 0].astype(jnp.float32)
        row_offsets = offsets[micro_index, 0]
        upstream = cotangent[micro_index, 0]
        upstream_f = upstream.astype(jnp.float32)
        angle = (row_offsets.astype(jnp.float32) * 0.25)[:, None] * frequency[None, :]
        cosine = jnp.cos(angle)
        sine_part = jnp.sin(angle)
        gathered = (
            lax.all_gather(w_query, ("dp", "seq"), axis=0, tiled=True),
            lax.all_gather(w_kv, ("dp", "seq"), axis=0, tiled=True),
            lax.all_gather(w_out, ("dp", "seq"), axis=0, tiled=True),
            lax.all_gather(w_up, ("dp", "seq"), axis=0, tiled=True),
            lax.all_gather(w_down, ("dp", "seq"), axis=0, tiled=True),
            lax.all_gather(b_up, ("dp", "seq"), axis=0, tiled=True),
            lax.all_gather(vectors, ("dp", "seq"), axis=1, tiled=True),
        )
        query_full, kv_full, out_full, up_full, down_full, up_bias, vector_full = gathered
        vector_f = vector_full.astype(jnp.float32)
        normed1, inverse1 = normalize(values_in)
        hidden1 = (normed1 * vector_f[0] + vector_f[1]).astype(jnp.bfloat16)
        query_pre = jnp.dot(hidden1, query_full, preferred_element_type=jnp.float32) + vector_f[4]
        kv_pre = jnp.dot(hidden1, kv_full, preferred_element_type=jnp.float32) + kv_bias
        queries = rotate(
            query_pre.reshape(local_rows, H, HD), cosine[:, None, :], sine_part[:, None, :]
        ).astype(jnp.bfloat16)
        shared_local = jnp.concatenate(
            [rotate(kv_pre[:, :HD], cosine, sine_part), kv_pre[:, HD:]], axis=1
        ).astype(jnp.bfloat16)
        shared = lax.all_gather(shared_local, "seq", axis=0, tiled=True)

        def block_scores(number):
            start_row = number * key_block
            key_piece = lax.dynamic_slice_in_dim(shared, start_row, key_block, 0)
            columns = start_row + jnp.arange(key_block, dtype=jnp.int32)
            allowed = (columns[None, :] <= row_ids[:, None]) & (
                row_ids[:, None] - columns[None, :] <= row_offsets[:, None]
            )
            scores = (
                jnp.einsum(
                    "rhd,kd->hrk", queries, key_piece[:, :HD], preferred_element_type=jnp.float32
                )
                * 0.125
            )
            return (jnp.where(allowed[None], scores, masked_score), key_piece)

        def max_step(number, state_pair):
            running_top, denominator = state_pair
            scores, key_piece = block_scores(number)
            new_top = jnp.maximum(running_top, jnp.max(scores, axis=-1))
            denominator = denominator * jnp.exp(running_top - new_top) + jnp.sum(
                jnp.exp(scores - new_top[..., None]), axis=-1
            )
            return (new_top, denominator)

        start_top = jnp.full((H, local_rows), masked_score, jnp.float32)
        running_top, denominator = lax.fori_loop(
            0, blocks_used, max_step, (start_top, jnp.zeros((H, local_rows), jnp.float32))
        )
        log_total = running_top + jnp.log(denominator)

        def value_step(number, accumulated):
            scores, key_piece = block_scores(number)
            soft_weights = jnp.exp(scores - log_total[..., None]).astype(jnp.bfloat16)
            return accumulated + jnp.einsum(
                "hrk,kd->rhd", soft_weights, key_piece[:, HD:], preferred_element_type=jnp.float32
            )

        attended_f = lax.fori_loop(
            0, blocks_used, value_step, jnp.zeros((local_rows, H, HD), jnp.float32)
        )
        attended = attended_f.reshape(local_rows, model_width).astype(jnp.bfloat16)
        attn_out = jnp.dot(attended, out_full, preferred_element_type=jnp.float32) + vector_f[5]
        normed2, inverse2 = normalize(values_in)
        hidden2 = (normed2 * vector_f[2] + vector_f[3]).astype(jnp.bfloat16)
        hidden_up = jnp.dot(hidden2, up_full, preferred_element_type=jnp.float32) + up_bias.astype(
            jnp.float32
        )
        activated = jax.nn.gelu(hidden_up, approximate=False).astype(jnp.bfloat16)
        mlp_out = jnp.dot(activated, down_full, preferred_element_type=jnp.float32) + vector_f[6]
        results.append((values_in + attn_out + mlp_out).astype(jnp.bfloat16))
        regathered = (
            lax.all_gather(w_query, ("dp", "seq"), axis=0, tiled=True),
            lax.all_gather(w_kv, ("dp", "seq"), axis=0, tiled=True),
            lax.all_gather(w_out, ("dp", "seq"), axis=0, tiled=True),
            lax.all_gather(w_up, ("dp", "seq"), axis=0, tiled=True),
            lax.all_gather(w_down, ("dp", "seq"), axis=0, tiled=True),
            lax.all_gather(b_up, ("dp", "seq"), axis=0, tiled=True),
            lax.all_gather(vectors, ("dp", "seq"), axis=1, tiled=True),
        )
        query_back, kv_back, out_back, up_back, down_back, up_bias_back, vector_back = regathered
        vector_back_f = vector_back.astype(jnp.float32)
        grad_w_down = jnp.einsum(
            "rf,rd->fd", activated, upstream, preferred_element_type=jnp.float32
        )
        d_act = jnp.einsum("rd,fd->rf", upstream, down_back, preferred_element_type=jnp.float32)
        d_hidden = (d_act * gelu_slope(hidden_up)).astype(jnp.bfloat16)
        grad_w_up = jnp.einsum("rd,rf->df", hidden2, d_hidden, preferred_element_type=jnp.float32)
        grad_b_up = jnp.sum(d_hidden.astype(jnp.float32), axis=0)
        d_normed2 = jnp.einsum("rf,df->rd", d_hidden, up_back, preferred_element_type=jnp.float32)
        grad_w_out = jnp.einsum("rd,re->de", attended, upstream, preferred_element_type=jnp.float32)
        d_attended = (
            jnp.einsum("re,de->rd", upstream, out_back, preferred_element_type=jnp.float32)
            .astype(jnp.bfloat16)
            .reshape(local_rows, H, HD)
        )

        def delta_step(number, accumulated):
            scores, key_piece = block_scores(number)
            soft_probs = jnp.exp(scores - log_total[..., None])
            d_probs = jnp.einsum(
                "rhd,kd->hrk", d_attended, key_piece[:, HD:], preferred_element_type=jnp.float32
            )
            return accumulated + jnp.sum(soft_probs * d_probs, axis=-1)

        delta = lax.fori_loop(0, blocks_used, delta_step, jnp.zeros((H, local_rows), jnp.float32))

        def grad_step(number, state_pair):
            d_query_rot, d_shared_all = state_pair
            start_row = number * key_block
            scores, key_piece = block_scores(number)
            soft_probs = jnp.exp(scores - log_total[..., None])
            d_probs = jnp.einsum(
                "rhd,kd->hrk", d_attended, key_piece[:, HD:], preferred_element_type=jnp.float32
            )
            d_scores = (soft_probs * (d_probs - delta[..., None])).astype(jnp.bfloat16)
            d_query_rot = (
                d_query_rot
                + jnp.einsum(
                    "hrk,kd->rhd", d_scores, key_piece[:, :HD], preferred_element_type=jnp.float32
                )
                * 0.125
            )
            d_keys = (
                jnp.einsum("hrk,rhd->kd", d_scores, queries, preferred_element_type=jnp.float32)
                * 0.125
            )
            d_values = jnp.einsum(
                "hrk,rhd->kd",
                soft_probs.astype(jnp.bfloat16),
                d_attended,
                preferred_element_type=jnp.float32,
            )
            current = lax.dynamic_slice_in_dim(d_shared_all, start_row, key_block, 0)
            d_shared_all = lax.dynamic_update_slice_in_dim(
                d_shared_all, current + jnp.concatenate([d_keys, d_values], axis=1), start_row, 0
            )
            return (d_query_rot, d_shared_all)

        d_query_rot, d_shared_all = lax.fori_loop(
            0,
            blocks_used,
            grad_step,
            (jnp.zeros((local_rows, H, HD), jnp.float32), jnp.zeros((seqlen, 2 * HD), jnp.float32)),
        )
        d_shared_mine = lax.psum_scatter(
            d_shared_all.astype(jnp.bfloat16), "seq", scatter_dimension=0, tiled=True
        ).astype(jnp.float32)
        d_shared = jnp.concatenate(
            [rotate(d_shared_mine[:, :HD], cosine, -sine_part), d_shared_mine[:, HD:]], axis=1
        ).astype(jnp.bfloat16)
        d_queries = (
            rotate(d_query_rot, cosine[:, None, :], -sine_part[:, None, :])
            .reshape(local_rows, model_width)
            .astype(jnp.bfloat16)
        )
        grad_w_query = jnp.einsum(
            "rd,re->de", hidden1, d_queries, preferred_element_type=jnp.float32
        )
        grad_w_kv = jnp.einsum("rd,rc->dc", hidden1, d_shared, preferred_element_type=jnp.float32)
        kv_bias_total = kv_bias_total + jnp.sum(d_shared.astype(jnp.float32), axis=0)
        d_normed1 = jnp.einsum(
            "re,de->rd", d_queries, query_back, preferred_element_type=jnp.float32
        ) + jnp.einsum("rc,dc->rd", d_shared, kv_back, preferred_element_type=jnp.float32)
        upstream_sum = jnp.sum(upstream_f, axis=0)
        grad_vectors = jnp.stack(
            [
                jnp.sum(d_normed1 * normed1, axis=0),
                jnp.sum(d_normed1, axis=0),
                jnp.sum(d_normed2 * normed2, axis=0),
                jnp.sum(d_normed2, axis=0),
                jnp.sum(d_queries.astype(jnp.float32), axis=0),
                upstream_sum,
                upstream_sum,
            ]
        )
        input_grads.append(
            upstream_f
            + norm_back(d_normed1, normed1, inverse1, vector_back_f[0])
            + norm_back(d_normed2, normed2, inverse2, vector_back_f[2])
        )
        shares = (
            lax.psum_scatter(grad_w_query, ("dp", "seq"), scatter_dimension=0, tiled=True),
            lax.psum_scatter(grad_w_kv, ("dp", "seq"), scatter_dimension=0, tiled=True),
            lax.psum_scatter(grad_w_out, ("dp", "seq"), scatter_dimension=0, tiled=True),
            lax.psum_scatter(grad_w_up, ("dp", "seq"), scatter_dimension=0, tiled=True),
            lax.psum_scatter(grad_w_down, ("dp", "seq"), scatter_dimension=0, tiled=True),
            lax.psum_scatter(grad_b_up, ("dp", "seq"), scatter_dimension=0, tiled=True),
            lax.psum_scatter(grad_vectors, ("dp", "seq"), scatter_dimension=1, tiled=True),
        )
        totals = shares if totals is None else tree_add(totals, shares)
    kv_bias_grad = lax.psum(kv_bias_total, ("dp", "seq"))
    return (
        jnp.stack(results)[:, None],
        jnp.stack(input_grads)[:, None],
        totals[0],
        totals[1],
        totals[2],
        totals[3],
        totals[4],
        totals[5],
        totals[6],
        kv_bias_grad,
    )


MESH = pl.DeviceIdType.MESH
NT = (((1,), (1,)), ((), ()))
VM = pl.BlockSpec(memory_space=pltpu.VMEM)
HBM = pl.BlockSpec(memory_space=pl.ANY)
GROUP = 4
KEYS = 512
MINI = 256
scale_log2 = 0.125 * 1.4426950408889634


def dot(left, right):
    return jnp.dot(left, right, preferred_element_type=jnp.float32)


def dot_nt(left, right):
    return lax.dot_general(left, right, NT, preferred_element_type=jnp.float32)


def bf(values):
    return values.astype(jnp.bfloat16)


def f32(values):
    return values.astype(jnp.float32)


def rotate_rows(block, cosine, sine_part):
    half_rot = ROT // 2
    first, second = block[:half_rot], block[half_rot:ROT]
    return jnp.concatenate(
        [first * cosine - second * sine_part, second * cosine + first * sine_part, block[ROT:]],
        axis=0,
    )


def here():
    return lax.axis_index("dp"), lax.axis_index("seq")


def greet(targets):
    barrier = pltpu.get_barrier_semaphore()
    for target in targets:
        pl.semaphore_signal(barrier, inc=1, device_id=target, device_id_type=MESH)
    pl.semaphore_wait(barrier, len(targets))


def remote(source, target, send, recv, device):
    return pltpu.make_async_remote_copy(
        src_ref=source,
        dst_ref=target,
        send_sem=send,
        recv_sem=recv,
        device_id=device,
        device_id_type=MESH,
    )


class Gather:
    def __init__(self, shard, slabs, halves, send, recv):
        self.shard, self.slabs, self.halves, self.send, self.recv = shard, slabs, halves, send, recv
        self.dp, self.seq = here()
        self.sent = []

    def index(self, dp_flip, z_flip, core_flip=0):
        return (self.dp ^ dp_flip) * 8 + (self.seq ^ (2 * z_flip + core_flip))

    def part(self, slab, half):
        rows, columns = half
        return self.slabs.at[slab, rows, columns]

    def start(self, number, source, target, device):
        remote(source, target, self.send.at[number], self.recv.at[number], device).start()
        self.sent.append(number)

    def arrived(self, number, target):
        remote(target, target, self.send.at[number], self.recv.at[number], (self.dp, self.seq ^ 1)).wait_recv()

    def along_z(self, flip):
        self.start(flip - 1, self.shard, self.slabs.at[self.index(0, 0)], (self.dp, self.seq ^ (2 * flip)))

    def own(self):
        mine = self.slabs.at[self.index(0, 0)]
        self.start(3, self.shard, mine, (self.dp ^ 1, self.seq))
        self.start(7, self.shard, mine, (self.dp ^ 2, self.seq))
        self.start(19, self.shard, mine, (self.dp, self.seq ^ 1))

    def from_z(self, flip):
        piece = self.slabs.at[self.index(0, flip)]
        self.arrived(flip - 1, piece)
        self.start(3 + flip, piece, piece, (self.dp ^ 1, self.seq))
        self.start(7 + flip, piece, piece, (self.dp ^ 2, self.seq))
        if flip == 2:
            self.start(2, piece, piece, (self.dp, self.seq ^ 2))
        self.start(19 + flip, piece, piece, (self.dp, self.seq ^ 1))

    def from_xy(self, flip):
        for axis, half in ((1, 0), (2, 1)):
            number = 3 if axis == 1 else 7
            slab = self.index(axis, flip)
            piece = self.slabs.at[slab]
            self.arrived(number + flip, piece)
            cut = self.part(slab, self.halves[half])
            self.start(11 + 4 * half + flip, cut, cut, (self.dp ^ (3 - axis), self.seq))
            self.start((23 if axis == 1 else 27) + flip, piece, piece, (self.dp, self.seq ^ 1))

    def from_diagonal(self, flip):
        slab = self.index(3, flip)
        for half in (0, 1):
            self.arrived(11 + 4 * half + flip, self.part(slab, self.halves[half]))
        piece = self.slabs.at[slab]
        self.start(31 + flip, piece, piece, (self.dp, self.seq ^ 1))

    def from_core(self):
        for number, dp_flip in ((19, 0), (23, 1), (27, 2), (31, 3)):
            for flip in range(4):
                self.arrived(number + flip, self.slabs.at[self.index(dp_flip, flip, 1)])

    def finish(self):
        for number in self.sent:
            view = self.part(0, self.halves[(number - 11) // 4]) if 11 <= number < 19 else self.slabs.at[0]
            remote(view, view, self.send.at[number], self.recv.at[number], (self.dp, self.seq ^ 1)).wait_send()


def attend(
    micro, steps, row0, off_ref, q_t, do_t, kv_ref, kv_t, att_t, dq_t, dkv, pair, scaled, score_ref, weight_ref, tick
):
    cols = slice(micro * MINI, (micro + 1) * MINI)
    row_ids = row0 + lax.broadcasted_iota(jnp.int32, (1, MINI), 1)
    begin = row_ids - off_ref[micro]

    def group_step(group, carry):
        heads = [pl.ds(pl.multiple_of((group * GROUP + n) * HD, HD), HD) for n in range(GROUP)]
        for n, head in enumerate(heads):
            pair[n, :HD, :MINI] = q_t[head, cols]
            pair[n, HD:, MINI:] = do_t[head, cols]

        def score_step(step, tops):
            keys = pl.ds(pl.multiple_of(step * KEYS, KEYS), KEYS)
            block = kv_ref[micro, keys, :]
            ids = step * KEYS + lax.broadcasted_iota(jnp.int32, (KEYS, 1), 0)
            allowed = (ids <= row_ids) & (ids >= begin)
            found = []
            for n in range(GROUP):
                both = dot(block, pair[n])
                scores = jnp.where(allowed, both[:, :MINI] * scale_log2, masked_score)
                score_ref[n, keys, :MINI] = scores
                score_ref[n, keys, MINI:] = both[:, MINI:]
                found.append(jnp.maximum(tops[n], jnp.max(scores.reshape(KEYS // 8, 8, MINI), axis=0)))
            return tuple(found)

        tops = lax.fori_loop(
            0, steps, score_step, tuple(jnp.full((8, MINI), masked_score, jnp.float32) for _ in heads)
        )
        tops = [jnp.max(top, axis=0, keepdims=True) for top in tops]
        tick(micro, group, 0)

        def value_step(step, carried):
            keys = pl.ds(pl.multiple_of(step * KEYS, KEYS), KEYS)
            values = kv_t[micro, HD:, keys]
            found = []
            for n in range(GROUP):
                output, total = carried[n]
                weights = jnp.exp2(score_ref[n, keys, :MINI] - tops[n])
                total = total + jnp.sum(weights.reshape(KEYS // 8, 8, MINI), axis=0)
                weight_ref[n, keys, :] = bf(weights)
                found.append((output + dot(values, bf(weights)), total))
            return tuple(found)

        sums = lax.fori_loop(
            0,
            steps,
            value_step,
            tuple((jnp.zeros((HD, MINI), jnp.float32), jnp.zeros((8, MINI), jnp.float32)) for _ in heads),
        )
        tick(micro, group, 1)
        inverses, deltas = [], []
        for n, head in enumerate(heads):
            inverse = 1.0 / jnp.sum(sums[n][1], axis=0, keepdims=True)
            output = sums[n][0] * inverse
            upstream = f32(do_t[head, cols])
            deltas.append(jnp.sum(output * upstream, axis=0, keepdims=True))
            inverses.append(inverse)
            att_t[head, cols] = bf(output)
            scaled[n, :HD, :MINI] = bf(f32(q_t[head, cols]) * inverse)
            scaled[n, HD:, MINI:] = bf(upstream * inverse)

        def grad_step(step, carried):
            keys = pl.ds(pl.multiple_of(step * KEYS, KEYS), KEYS)
            key_block = kv_t[micro, :HD, keys]
            total = dkv[micro, keys, :]
            found = []
            for n in range(GROUP):
                weights = weight_ref[n, keys, :]
                d_scores = bf(f32(weights) * (score_ref[n, keys, MINI:] - deltas[n]))
                found.append(carried[n] + dot(key_block, d_scores))
                total = total + dot_nt(d_scores, scaled[n, :, :MINI])
                total = total + dot_nt(weights, scaled[n, :, MINI:])
            dkv[micro, keys, :] = total
            return tuple(found)

        grads = lax.fori_loop(
            0, steps, grad_step, tuple(jnp.zeros((HD, MINI), jnp.float32) for _ in heads)
        )
        for n, head in enumerate(heads):
            dq_t[head, cols] = grads[n] * (inverses[n] * 0.125)
        tick(micro, group, 2)
        return carry

    lax.fori_loop(0, H // GROUP, group_step, 0)


def spread(slabs):
    lane = lax.broadcasted_iota(jnp.int32, (8, 128), 1)
    row = lax.broadcasted_iota(jnp.int32, (8, 128), 0)
    rows = [jnp.zeros((8, 128), jnp.float32) for _ in range(6)]
    wide = [jnp.zeros((8, 128), jnp.float32) for _ in range(24)]
    for number in range(32):
        for width, target, keep in ((24, rows, row < 7), (96, wide, row == 7)):
            block, shift = divmod(number * width, 128)
            piece = jnp.where(keep, slabs[number], 0.0)
            piece = pltpu.roll(piece, shift, 1) if shift else piece
            target[block] = target[block] + jnp.where(lane >= shift, piece, 0.0)
            if shift + width > 128:
                target[block + 1] = target[block + 1] + jnp.where(lane < shift, piece, 0.0)
    return jnp.concatenate(rows, axis=1), jnp.concatenate(wide, axis=1)


def slab_order(store, block, dp_index, rows):
    for z in range(4):
        for core in range(2):
            first = (2 * z + core) * rows
            store(dp_index, core, z, bf(block[first : first + rows]))


def attention_kernel(
    x_ref, cot_ref, off_ref, wq_ref, wkv_in, wout_ref, vec_in, bup_in, bkv_ref, up_ref, down_ref,
    up_slabs, down_slabs, vec_ref, bup_ref, wkv_ref, cos_ref, sin_ref, attn_ref, dn_ref, dkv_out, grads_ref, dqsum_ref,
    small_ref, pair_ref, extra, slabs, pair_slabs, weights, out_weights, n1t_ref, q_t, do_t, att_t, dq_t, kv_ref, kv_t, dkv, pair, scaled,
    score_ref, weight_ref,
    send_a, recv_a, send_o, recv_o, send_u, recv_u, send_d, recv_d, send_kv, recv_kv, local_sem,
):
    dp, seq = here()

    def halves(shape, axis):
        middle = shape[axis] // 2
        cuts = [slice(0, middle), slice(middle, 2 * middle)]
        return tuple((cut, slice(None)) if axis == 0 else (slice(None), cut) for cut in cuts)

    gather_a = Gather(small_ref, slabs, halves(small_ref.shape, 1), send_a, recv_a)
    gather_o = Gather(pair_ref, pair_slabs, halves(pair_ref.shape, 1), send_o, recv_o)
    gather_u = Gather(up_ref, up_slabs, halves(up_ref.shape, 1), send_u, recv_u)
    gather_d = Gather(down_ref, down_slabs, halves(down_ref.shape, 0), send_d, recv_d)

    def signal():
        barrier = pltpu.get_barrier_semaphore()
        for target in friends:
            pl.semaphore_signal(barrier, inc=1, device_id=target, device_id_type=MESH)

    friends = [(dp, seq ^ 1), (dp, seq ^ 2), (dp, seq ^ 4), (dp, seq ^ 6), (dp ^ 1, seq), (dp ^ 2, seq)]
    signal()
    extra[...] = jnp.zeros_like(extra)
    extra[0:7, 0 : vec_in.shape[1]] = f32(vec_in[...])
    extra[7:8, 0 : bup_in.shape[1]] = f32(bup_in[...])
    small_ref[:, 0:128] = wkv_in[...]
    small_ref[:, 128:256] = bf(extra[...])
    pair_ref[:, 0:768] = wq_ref[...]
    pair_ref[:, 768:1536] = wout_ref[...]
    pl.semaphore_wait(pltpu.get_barrier_semaphore(), len(friends))
    for flip in (1, 2):
        gather_a.along_z(flip)
    gather_a.own()
    gather_o.along_z(1)
    gather_o.own()
    gather_u.own()
    mine = gather_a.index(0, 0)
    local_copies = [
        pltpu.make_async_copy(small_ref, slabs.at[mine], local_sem.at[0]),
        pltpu.make_async_copy(pair_ref, pair_slabs.at[mine], local_sem.at[1]),
        pltpu.make_async_copy(up_ref, up_slabs.at[mine], local_sem.at[2]),
        pltpu.make_async_copy(down_ref, down_slabs.at[mine], local_sem.at[3]),
    ]
    for copy in local_copies:
        copy.start()
    pair[...] = jnp.zeros_like(pair)
    scaled[...] = jnp.zeros_like(scaled)
    dkv[...] = jnp.zeros_like(dkv)
    rank = f32(lax.broadcasted_iota(jnp.int32, (ROT // 2, 1), 0))
    frequency = jnp.exp(rank * (-2.0 / ROT * math.log(10000.0)))
    for micro in range(2):
        cols = slice(micro * MINI, (micro + 1) * MINI)
        angle = (f32(off_ref[micro]) * 0.25) * frequency
        cos_ref[:, cols] = jnp.cos(angle)
        sin_ref[:, cols] = jnp.sin(angle)
    normed, _ = normalize(f32(x_ref[...]))
    for flip in (1, 2, 3):
        gather_a.from_z(flip)
    for flip in range(4):
        gather_a.from_xy(flip)
    gather_o.along_z(2)
    gather_o.from_z(1)
    for flip in range(4):
        gather_a.from_diagonal(flip)
    gather_o.from_xy(0)
    gather_u.along_z(1)
    gather_u.along_z(2)
    gather_a.from_core()
    local_copies[0].wait()

    vectors, wide_row = spread([f32(slabs[number, 0:8, 128:256]) for number in range(32)])
    vec_ref[...] = vectors
    bup_ref[...] = wide_row[7:8]

    def unpack(source, target, columns):
        for number in range(16):
            block = jnp.concatenate(
                [f32(source[2 * number, :, columns]), f32(source[2 * number + 1, :, columns])], axis=0
            )
            target[48 * number : 48 * number + 48, :] = bf(block)

    unpack(slabs, wkv_ref, slice(0, 128))
    hidden = bf(normed * vectors[0:1] + vectors[1:2])
    kv_pre = dot(hidden, wkv_ref[...]) + f32(bkv_ref[...])
    kv_pre_t = kv_pre.T
    cosine, sine_part = cos_ref[...], sin_ref[...]
    shared_t = bf(jnp.concatenate([rotate_rows(kv_pre_t[:HD], cosine, sine_part), kv_pre_t[HD:]], axis=0))
    shared = bf(f32(shared_t).T)
    place = pl.ds(pl.multiple_of(seq * MINI, MINI), MINI)
    kv_copies = []
    for micro in range(2):
        kv_ref[micro, place, :] = shared[micro * MINI : (micro + 1) * MINI]

    def kv_block(micro, flip):
        return kv_ref.at[micro, pl.ds(pl.multiple_of((seq ^ flip) * MINI, MINI), MINI)]

    def kv_send(micro, flip, number, device):
        block = kv_block(micro, flip)
        copy = remote(block, block, send_kv.at[micro, number], recv_kv.at[micro, number], device)
        copy.start()
        kv_copies.append(copy)

    def kv_arrived(micro, flip, number):
        block = kv_block(micro, flip)
        remote(block, block, send_kv.at[micro, number], recv_kv.at[micro, number], (dp, seq ^ 1)).wait_recv()

    def kv_start(micro):
        for flip in (1, 2, 3):
            kv_send(micro, 0, flip - 1, (dp, seq ^ (2 * flip)))
        kv_send(micro, 0, 3, (dp, seq ^ 1))

    def kv_forward(micro):
        for flip in (1, 2, 3):
            kv_arrived(micro, 2 * flip, flip - 1)
            kv_send(micro, 2 * flip, 3 + flip, (dp, seq ^ 1))

    def kv_finish(micro):
        for flip in range(4):
            kv_arrived(micro, 2 * flip + 1, 3 + flip)
        kv_t[micro] = bf(f32(kv_ref[micro]).T)

    kv_start(0)
    gather_o.from_z(2)
    gather_o.from_xy(1)
    gather_o.from_diagonal(0)
    gather_o.from_z(3)
    gather_o.from_xy(2)
    gather_o.from_diagonal(1)
    n1t_ref[...] = bf(f32(hidden).T)
    kv_forward(0)
    gather_o.from_xy(3)
    gather_d.along_z(1)
    gather_d.along_z(2)
    gather_d.own()
    gather_u.from_z(1)
    gather_u.from_xy(0)
    gather_o.from_diagonal(2)
    gather_o.from_diagonal(3)
    kv_start(1)
    kv_finish(0)
    local_copies[1].wait()
    gather_o.from_core()
    unpack(pair_slabs, weights, slice(0, 768))
    unpack(pair_slabs, out_weights, slice(768, 1536))
    query = (dot(hidden, weights[...]) + vectors[4:5]).T
    for head in range(H):
        q_t[head * HD : (head + 1) * HD, :] = bf(
            rotate_rows(query[head * HD : (head + 1) * HD], cosine, sine_part)
        )
    do_t[...] = bf(dot_nt(out_weights[...], cot_ref[...]))

    def each(name, *flips):
        def act():
            for gather in (gather_u, gather_d):
                for flip in flips:
                    getattr(gather, name)(flip)

        return act

    def then(*acts):
        def act():
            for one in acts:
                one()

        return act

    actions = [
        lambda: gather_d.from_z(1),
        lambda: gather_d.from_xy(0),
        None,
        then(each("from_z", 2), lambda: gather_u.from_diagonal(0)),
        each("from_xy", 1),
        lambda: gather_d.from_diagonal(0),
        each("from_z", 3),
        each("from_diagonal", 1),
        each("from_xy", 2),
        None,
        each("from_diagonal", 2),
        None,
        each("from_xy", 3),
        None,
        None,
        each("from_diagonal", 3),
        None,
        None,
    ]

    def tick(micro, group, part):
        for number in range(H // GROUP):
            act = actions[(micro * (H // GROUP) + number) * 3 + part]
            if act is not None:
                pl.when(group == number)(act)

    kv_forward(1)
    steps = lax.div((seq + 1) * MINI + KEYS - 1, KEYS)
    for micro in range(2):
        if micro == 1:
            kv_finish(1)
        attend(
            micro, steps, seq * MINI, off_ref, q_t, do_t, kv_ref, kv_t, att_t, dq_t, dkv,
            pair, scaled, score_ref, weight_ref, tick,
        )
    for micro in range(2):
        for core in range(2):
            for z in range(4):
                first = (2 * z + core) * MINI
                block = dkv[micro, first : first + MINI, :]
                scale = jnp.where(lax.broadcasted_iota(jnp.int32, (1, 2 * HD), 1) < HD, 0.125, 1.0)
                dkv_out[core, z, micro] = bf(block * scale)
    attn_ref[...] = dot(bf(f32(att_t[...]).T), out_weights[...]) + vectors[5:6]
    for head in range(H):
        dq_t[head * HD : (head + 1) * HD, :] = rotate_rows(
            dq_t[head * HD : (head + 1) * HD, :], cosine, -sine_part
        )
    d_query = bf(dq_t[...].T)
    dqsum_ref[...] = jnp.sum(f32(d_query), axis=0, keepdims=True)
    dn_ref[...] = dot_nt(d_query, weights[...])
    for block in range(4):
        rows = slice(192 * block, 192 * block + 192)

        def put_query(dp_index, core, z, piece):
            grads_ref[dp_index, core, z, :, 0:768] = piece

        def put_out(dp_index, core, z, piece):
            grads_ref[dp_index, core, z, :, 768:1536] = piece

        slab_order(put_query, dot(n1t_ref[rows, :], d_query), block, 24)
        slab_order(put_out, dot(att_t[rows, :], cot_ref[...]), block, 24)
    for gather in (gather_u, gather_d):
        gather.from_core()
    for gather in (gather_a, gather_o, gather_u, gather_d):
        gather.finish()
    for copy in kv_copies:
        copy.wait_send()
    for copy in local_copies[2:]:
        copy.wait()


def attention_call(x, cot, offsets, w_query, w_kv, w_out, vectors, b_up, b_kv, w_up, w_down):
    rows = x.shape[0]
    dma = pltpu.SemaphoreType.DMA
    out = jax.ShapeDtypeStruct
    seqlen = 8 * MINI
    b16 = jnp.bfloat16
    return pl.pallas_call(
        attention_kernel,
        out_shape=(
            out((32,) + w_up.shape, b16),
            out((32,) + w_down.shape, b16),
            out((8, 768), jnp.float32),
            out((1, 3072), jnp.float32),
            out((768, 128), b16),
            out((ROT // 2, rows), jnp.float32),
            out((ROT // 2, rows), jnp.float32),
            out((rows, 768), jnp.float32),
            out((rows, 768), jnp.float32),
            out((2, 4, 2, MINI, 2 * HD), b16),
            out((4, 2, 4, 24, 1536), b16),
            out((1, 768), jnp.float32),
        ),
        in_specs=[VM] * 9 + [HBM] * 2,
        out_specs=(HBM, HBM) + (VM,) * 10,
        scratch_shapes=[
            pltpu.VMEM((24, 256), b16),
            pltpu.VMEM((24, 1536), b16),
            pltpu.VMEM((24, 128), jnp.float32),
            pltpu.VMEM((32, 24, 256), b16),
            pltpu.VMEM((32, 24, 1536), b16),
            pltpu.VMEM((768, 768), b16),
            pltpu.VMEM((768, 768), b16),
            pltpu.VMEM((768, rows), b16),
            pltpu.VMEM((768, rows), b16),
            pltpu.VMEM((768, rows), b16),
            pltpu.VMEM((768, rows), b16),
            pltpu.VMEM((768, rows), jnp.float32),
            pltpu.VMEM((2, seqlen, 2 * HD), b16),
            pltpu.VMEM((2, 2 * HD, seqlen), b16),
            pltpu.VMEM((2, seqlen, 2 * HD), jnp.float32),
            pltpu.VMEM((GROUP, 2 * HD, 2 * MINI), b16),
            pltpu.VMEM((GROUP, 2 * HD, 2 * MINI), b16),
            pltpu.VMEM((GROUP, seqlen, 2 * MINI), jnp.float32),
            pltpu.VMEM((GROUP, seqlen, MINI), b16),
        ]
        + [dma((35,))] * 8
        + [dma((2, 7))] * 2
        + [dma((4,))],
        compiler_params=pltpu.CompilerParams(
            collective_id=0, has_side_effects=True, vmem_limit_bytes=60 << 20
        ),
        name="attention",
    )(x, cot, offsets, w_query, w_kv, w_out, vectors, b_up, b_kv, w_up, w_down)


def packed_on_device(inputs, offsets, w_query, w_kv, w_out, w_up, w_down, b_up, vectors, b_kv, cotangent):
    rows = 2 * MINI
    x = inputs.reshape(rows, 768)
    cot = cotangent.reshape(rows, 768)
    up_slabs, down_slabs, vec, bup, wkv, cosine, sine_part, attn, dn1, dkv, grads_a, dq_sum = attention_call(
        x, cot, offsets, w_query, w_kv, w_out, vectors, b_up.reshape(1, -1), b_kv.reshape(1, -1), w_up, w_down
    )
    return feed_forward(x, cot, cosine, sine_part, up_slabs, down_slabs, vec, bup, wkv, attn, dn1, dkv, grads_a, dq_sum)


class Scatter:
    def __init__(self, slabs, from_core, from_diagonal, from_xy, from_z, send, recv):
        self.slabs, self.from_core, self.from_diagonal = slabs, from_core, from_diagonal
        self.from_xy, self.from_z, self.send, self.recv = from_xy, from_z, send, recv
        self.dp, self.seq = here()
        self.core = lax.rem(self.seq, 2)
        self.z = lax.div(self.seq, 2)
        self.sent = []

    def start(self, number, source, target, device):
        copy = remote(source, target, self.send.at[number], self.recv.at[number], device)
        copy.start()
        self.sent.append(copy)

    def arrived(self, number, target):
        remote(target, target, self.send.at[number], self.recv.at[number], (self.dp, self.seq ^ 1)).wait_recv()

    def block(self, flip):
        return self.slabs.at[self.dp ^ flip, self.core]

    def to_core(self, flip):
        other = self.slabs.at[self.dp ^ flip, 1 - self.core]
        self.start(flip, other, self.from_core.at[flip], (self.dp, self.seq ^ 1))

    def add(self, block, z, terms):
        total = f32(block[z])
        for term in terms:
            total = total + f32(term)
        block[z] = bf(total)

    def diagonal(self):
        block = self.block(3)
        self.arrived(3, self.from_core.at[3])
        for half in (0, 1):
            for z in (2 * half, 2 * half + 1):
                self.add(block, z, [self.from_core[3, z]])
            self.start(4 + half, block.at[pl.ds(2 * half, 2)], self.from_diagonal.at[half], (self.dp ^ (1 + half), self.seq))

    def beside(self, axis):
        half = 2 - axis
        block = self.block(axis)
        self.arrived(axis, self.from_core.at[axis])
        self.arrived(4 + half, self.from_diagonal.at[half])
        for z in range(4):
            terms = [self.from_core[axis, z]]
            if z // 2 == half:
                terms.append(self.from_diagonal[half, z % 2])
            self.add(block, z, terms)
        self.start(5 + axis, block, self.from_xy.at[axis - 1], (self.dp ^ axis, self.seq))

    def own(self):
        block = self.block(0)
        self.arrived(0, self.from_core.at[0])
        for axis in (1, 2):
            self.arrived(5 + axis, self.from_xy.at[axis - 1])
        for z in range(4):
            self.add(block, z, [self.from_core[0, z], self.from_xy[0, z], self.from_xy[1, z]])
        for flip in (1, 2, 3):
            self.start(7 + flip, block.at[self.z ^ flip], self.from_z.at[flip - 1], (self.dp, self.seq ^ (2 * flip)))

    def total(self):
        value = f32(self.slabs[self.dp, self.core, self.z])
        for flip in (1, 2, 3):
            self.arrived(7 + flip, self.from_z.at[flip - 1])
            value = value + f32(self.from_z[flip - 1])
        return value

    def finish(self):
        for copy in self.sent:
            copy.wait_send()


def feed_kernel(
    x_ref, cot_ref, cos_ref, sin_ref, vec_ref, bup_ref, wkv_ref, attn_ref, dn_ref, dqsum_ref, dkv_in, grads_a, up_hbm, down_hbm,
    out_ref, gin_ref, gq_ref, go_ref, gu_ref, gkv_ref, gd_ref, small_out,
    up_ref, down_ref, n1t_ref, n2_ref, n2t_ref, act_ref, dh_ref, mlp_ref, dshared_ref, stats,
    a_slabs, d_slabs, u_slabs, v_slabs,
    a_core, a_diag, a_xy, a_z, d_core, d_diag, d_xy, d_z, u_core, u_diag, u_xy, u_z, v_core, v_diag, v_xy, v_z,
    dkv, dkv_core, dkv_z, small, small_in,
    send_s, recv_s, send_k, recv_k, send_m, recv_m, load_sem,
):
    dp, seq = here()
    core, z = lax.rem(seq, 2), lax.div(seq, 2)
    loads = [
        pltpu.make_async_copy(dkv_in, dkv, load_sem.at[2]),
        pltpu.make_async_copy(grads_a, a_slabs, load_sem.at[3]),
        pltpu.make_async_copy(up_hbm, up_ref, load_sem.at[0]),
        pltpu.make_async_copy(down_hbm, down_ref, load_sem.at[1]),
    ]
    for copy in loads:
        copy.start()
    greet(
        [(dp, seq ^ 1), (dp, seq ^ 2), (dp, seq ^ 4), (dp, seq ^ 6), (dp ^ 1, seq), (dp ^ 2, seq)]
    )
    scatter_a = Scatter(a_slabs, a_core, a_diag, a_xy, a_z, send_s.at[0], recv_s.at[0])
    scatter_d = Scatter(d_slabs, d_core, d_diag, d_xy, d_z, send_s.at[1], recv_s.at[1])
    scatter_u = Scatter(u_slabs, u_core, u_diag, u_xy, u_z, send_s.at[2], recv_s.at[2])
    scatter_v = Scatter(v_slabs, v_core, v_diag, v_xy, v_z, send_s.at[3], recv_s.at[3])
    kv_sent = []

    def kv_start(number, source, target, device):
        copy = remote(source, target, send_k.at[number], recv_k.at[number], device)
        copy.start()
        kv_sent.append(copy)

    def kv_arrived(number, target):
        remote(target, target, send_k.at[number], recv_k.at[number], (dp, seq ^ 1)).wait_recv()

    loads[1].wait()
    for flip in (3, 1, 2, 0):
        scatter_a.to_core(flip)
    loads[0].wait()
    kv_start(0, dkv.at[1 - core], dkv_core, (dp, seq ^ 1))
    scatter_a.diagonal()

    vectors = vec_ref[...]
    for start in range(0, 2 * MINI, MINI):
        rows = slice(start, start + MINI)
        normed, inverse = normalize(f32(x_ref[rows, :]))
        stats[rows, :] = jnp.broadcast_to(inverse, (MINI, 128))
        n1t_ref[:, rows] = bf((normed * vectors[0:1] + vectors[1:2]).T)
        second = normed * vectors[2:3] + vectors[3:4]
        n2_ref[rows, :] = bf(second)
        n2t_ref[:, rows] = bf(second.T)
    kv_arrived(0, dkv_core)
    for index in range(4):
        for micro in range(2):
            dkv[core, index, micro] = bf(f32(dkv[core, index, micro]) + f32(dkv_core[index, micro]))
    for flip in (1, 2, 3):
        kv_start(flip, dkv.at[core, z ^ flip], dkv_z.at[flip - 1], (dp, seq ^ (2 * flip)))
    scatter_a.beside(1)
    scatter_a.beside(2)
    loads[2].wait()
    loads[3].wait()

    def chunk(flip, first):
        base = (dp ^ flip) * 768

        def tile(number, carry):
            columns = pl.ds(pl.multiple_of(base + number * 256, 256), 256)
            hidden = dot(n2_ref[...], up_ref[:, columns]) + bup_ref[0:1, columns]
            d_act = dot_nt(cot_ref[...], down_ref[columns, :])
            normal = 0.5 + 0.5 * lax.erf(hidden * root_half)
            density = density_scale * jnp.exp(-0.5 * hidden * hidden)
            d_hidden = bf(d_act * (normal + hidden * density))
            act_ref[:, pl.ds(pl.multiple_of(number * 256, 256), 256)] = bf(hidden * normal)
            dh_ref[:, columns] = d_hidden
            return carry

        lax.fori_loop(0, 3, tile, 0)
        down_rows = pl.ds(pl.multiple_of(base, 768), 768)
        part = dot(act_ref[...], down_ref[down_rows, :])
        mlp_ref[...] = part if first else mlp_ref[...] + part

        grad_t = bf(f32(act_ref[...]).T)
        for number in range(4):
            grad = dot(grad_t[192 * number : 192 * number + 192], cot_ref[...])
            for half in range(2):
                d_slabs[dp ^ flip, half, number] = bf(grad[96 * half : 96 * half + 96])
        scatter_d.to_core(flip)

    def put(store, block, flip, rows):
        for index in range(4):
            for half in range(2):
                first = (2 * index + half) * rows
                store(dp ^ flip, half, index, bf(block[first : first + rows]))

    def up_block(flip, left):
        rows = pl.ds(pl.multiple_of((dp ^ flip) * 192, 192), 192)
        if left:

            def put_left(target, half, index, piece):
                u_slabs[target, half, index, :, 0:1536] = piece

            def put_kv(target, half, index, piece):
                u_slabs[target, half, index, :, 1536:1664] = piece

            put(put_left, dot(n2t_ref[rows, :], dh_ref[:, 0:1536]), flip, 24)
            put(put_kv, dot(n1t_ref[rows, :], dshared_ref[...]), flip, 24)
            scatter_u.to_core(flip)
        else:

            def put_right(target, half, index, piece):
                v_slabs[target, half, index] = piece

            put(put_right, dot(n2t_ref[rows, :], dh_ref[:, 1536:3072]), flip, 24)
            scatter_v.to_core(flip)

    chunk(3, True)
    scatter_d.diagonal()
    chunk(1, False)
    scatter_a.own()
    scatter_d.beside(1)
    for flip in (1, 2, 3):
        kv_arrived(flip, dkv_z.at[flip - 1])
    cosine, sine_part = cos_ref[...], sin_ref[...]
    for micro in range(2):
        cols = slice(micro * MINI, (micro + 1) * MINI)
        total = f32(dkv[core, z, micro])
        for flip in (1, 2, 3):
            total = total + f32(dkv_z[flip - 1, micro])
        total_t = total.T
        total_t = jnp.concatenate(
            [rotate_rows(total_t[:HD], cosine[:, cols], -sine_part[:, cols]), total_t[HD:]], axis=0
        )
        dshared_ref[cols, :] = bf(total_t.T)
    chunk(2, False)
    scatter_d.beside(2)
    chunk(0, False)
    up_block(3, True)
    up_block(1, True)
    scatter_u.diagonal()
    up_block(2, True)
    up_block(0, True)
    scatter_d.own()
    up_block(3, False)
    up_block(1, False)
    scatter_u.beside(1)
    scatter_u.beside(2)
    scatter_v.diagonal()
    up_block(2, False)
    up_block(0, False)
    zero = jnp.zeros((1, 768), jnp.float32)
    sums = [zero] * 5
    for start in range(0, 2 * MINI, 128):
        rows = slice(start, start + 128)
        values = f32(x_ref[rows, :])
        upstream = f32(cot_ref[rows, :])
        inverse = stats[rows, 0:1]
        normed = (values - jnp.mean(values, axis=-1, keepdims=True)) * inverse
        out_ref[rows, :] = bf(values + attn_ref[rows, :] + mlp_ref[rows, :] + vectors[6:7])
        first = dn_ref[rows, :] + dot_nt(dshared_ref[rows, :], wkv_ref[...])
        second = dot_nt(dh_ref[rows, :], up_ref[...])
        gin_ref[rows, :] = (
            upstream
            + norm_back(first, normed, inverse, vectors[0:1])
            + norm_back(second, normed, inverse, vectors[2:3])
        )
        news = (first * normed, first, second * normed, second, upstream)
        sums = [total + jnp.sum(new, axis=0, keepdims=True) for total, new in zip(sums, news)]
    b_up_sum = jnp.sum(f32(dh_ref[...]), axis=0, keepdims=True)
    kv_sum = jnp.sum(f32(dshared_ref[...]), axis=0, keepdims=True)
    small[0] = jnp.concatenate(
        sums[:4]
        + [dqsum_ref[...], sums[4], sums[4], zero]
        + [b_up_sum[:, 768 * n : 768 * n + 768] for n in range(4)]
        + [jnp.concatenate([kv_sum, zero[:, 128:]], axis=1)]
        + [zero] * 3,
        axis=0,
    )
    partners = [(dp, seq ^ 1), (dp, seq ^ 2), (dp, seq ^ 4), (dp ^ 1, seq), (dp ^ 2, seq)]
    small_sent = []

    def small_start(number):
        copy = remote(small.at[number], small_in.at[number], send_m.at[number], recv_m.at[number], partners[number])
        copy.start()
        small_sent.append(copy)

    def small_end(number):
        small_sent[number].wait_recv()
        small[number + 1] = small[number] + small_in[number]

    total = scatter_a.total()
    gq_ref[...] = total[:, :768]
    go_ref[...] = total[:, 768:]
    small_start(0)
    scatter_v.beside(1)
    scatter_v.beside(2)
    small_end(0)
    small_start(1)
    scatter_u.own()
    small_end(1)
    small_start(2)
    gd_ref[...] = scatter_d.total()
    scatter_v.own()
    small_end(2)
    small_start(3)
    total = scatter_u.total()
    gu_ref[:, 0:1536] = total[:, 0:1536]
    gkv_ref[...] = total[:, 1536:1664]
    small_end(3)
    small_start(4)
    small_end(4)
    small_out[...] = small[5]
    gu_ref[:, 1536:3072] = scatter_v.total()
    for scatter in (scatter_a, scatter_d, scatter_u, scatter_v):
        scatter.finish()
    for copy in kv_sent + small_sent:
        copy.wait_send()


def place_kernel(small, *refs):
    wholes, results = refs[:7], refs[7:17]
    for source, target in zip(wholes, results):
        target[...] = source[...]
    dp, seq = here()
    rows = small[0:8, :]
    shift = lax.rem(768 - 24 * (8 * dp + seq), 768)
    results[7][...] = pltpu.roll(rows, shift, 1)[0:7, 0:24]
    wide = jnp.broadcast_to(small[pl.ds(8 + dp, 1), :], (8, 768))
    shift = lax.rem(768 - 96 * seq, 768)
    results[8][...] = pltpu.roll(wide, shift, 1)[0:1, 0:96]
    results[9][...] = small[12:13, 0 : 2 * HD]


def feed_forward(x, cot, cosine, sine_part, up_slabs, down_slabs, vec, bup, wkv, attn, dn1, dkv, grads_a, dq_sum):
    rows = x.shape[0]
    dma = pltpu.SemaphoreType.DMA
    out = jax.ShapeDtypeStruct
    b16 = jnp.bfloat16
    shapes = ((24, 1536), (96, 768), (24, 1664), (24, 1536))
    buffers = [pltpu.VMEM((4, 2, 4) + shape, b16) for shape in shapes]
    for shape in shapes:
        for lead in ((4, 4), (2, 2), (2, 4), (3,)):
            buffers.append(pltpu.VMEM(lead + shape, b16))
    out_rows, g_in, g_query, g_out, g_up, g_kv, g_down, small = pl.pallas_call(
        feed_kernel,
        out_shape=(
            out((rows, 768), b16),
            out((rows, 768), jnp.float32),
            out((24, 768), jnp.float32),
            out((24, 768), jnp.float32),
            out((24, 3072), jnp.float32),
            out((24, 128), jnp.float32),
            out((96, 768), jnp.float32),
            out((16, 768), jnp.float32),
        ),
        in_specs=[VM] * 10 + [HBM] * 4,
        out_specs=(VM,) * 8,
        scratch_shapes=[
            pltpu.VMEM((768, 3072), b16),
            pltpu.VMEM((3072, 768), b16),
            pltpu.VMEM((768, rows), b16),
            pltpu.VMEM((rows, 768), b16),
            pltpu.VMEM((768, rows), b16),
            pltpu.VMEM((rows, 768), b16),
            pltpu.VMEM((rows, 3072), b16),
            pltpu.VMEM((rows, 768), jnp.float32),
            pltpu.VMEM((rows, 2 * HD), b16),
            pltpu.VMEM((rows, 128), jnp.float32),
        ]
        + buffers
        + [
            pltpu.VMEM((2, 4, 2, MINI, 2 * HD), b16),
            pltpu.VMEM((4, 2, MINI, 2 * HD), b16),
            pltpu.VMEM((3, 2, MINI, 2 * HD), b16),
            pltpu.VMEM((6, 16, 768), jnp.float32),
            pltpu.VMEM((5, 16, 768), jnp.float32),
            dma((4, 11)),
            dma((4, 11)),
            dma((4,)),
            dma((4,)),
            dma((5,)),
            dma((5,)),
            dma((4,)),
        ],
        compiler_params=pltpu.CompilerParams(
            collective_id=1, has_side_effects=True, vmem_limit_bytes=63 << 20
        ),
        name="feed_forward",
    )(
        x, cot, cosine, sine_part, vec, bup, wkv, attn, dn1, dq_sum, dkv, grads_a,
        up_slabs.reshape(768, 3072), down_slabs.reshape(3072, 768),
    )
    wholes = (out_rows, g_in, g_query, g_kv, g_out, g_up, g_down)
    like = tuple(out(one.shape, one.dtype) for one in wholes)
    results = pl.pallas_call(
        place_kernel,
        out_shape=like + (out((7, 24), jnp.float32), out((1, 96), jnp.float32), out((1, 2 * HD), jnp.float32)),
        in_specs=[VM] * (1 + len(wholes)),
        out_specs=(VM,) * (3 + len(wholes)),
        compiler_params=pltpu.CompilerParams(vmem_limit_bytes=62 << 20),
        name="place",
    )(small, *wholes)
    out_rows, g_in, g_query, g_kv, g_out, g_up, g_down, g_vectors, g_b_up, g_b_kv = results
    return (
        out_rows.reshape(2, 1, MINI, 768), g_in.reshape(2, 1, MINI, 768), g_query, g_kv, g_out,
        g_up, g_down, g_b_up.reshape(-1), g_vectors, g_b_kv.reshape(-1),
    )


def solution(mesh):
    packed = mesh.shape["dp"] == 4 and mesh.shape["seq"] == 8
    on_device = packed_on_device if packed else plain_on_device

    in_specs = (
        P(None, "dp", "seq", None),
        P(None, "dp", "seq"),
        P(("dp", "seq"), None),
        P(("dp", "seq"), None),
        P(("dp", "seq"), None),
        P(("dp", "seq"), None),
        P(("dp", "seq"), None),
        P(("dp", "seq")),
        P(None, ("dp", "seq")),
        P(),
        P(None, "dp", "seq", None),
    )
    out_specs = (
        P(None, "dp", "seq", None),
        P(None, "dp", "seq", None),
        P(("dp", "seq"), None),
        P(("dp", "seq"), None),
        P(("dp", "seq"), None),
        P(("dp", "seq"), None),
        P(("dp", "seq"), None),
        P(("dp", "seq")),
        P(None, ("dp", "seq")),
        P(),
    )
    return jax.shard_map(
        on_device, mesh=mesh, in_specs=in_specs, out_specs=out_specs, check_vma=False
    )
```

profile of v0, /device:TPU:0, one launch (start us, length us, event | category | flops | bytes accessed | tf_op | source)
XLA Modules:
  0.0 191.3 jit_solution(8756563692582404392)
XLA Ops:
  0.6 84.6 %attention.1 = (bf16[32,24,3072]{2,1,0:T(8,128)(2,1)}, bf16[32,96,768]{2,1,0:T(8,128)(2,1)}, f32[8,768]{1,0:T(8,128)}, f32[1,3072]{1,0:T(1,128)}, bf16[768,128]{...) custom-call(bf16[512,768]{1,0:T(8,128)(2,1)} %bitcast.16, ...), custom_call_target="tpu_custom_call" | custom-call | tf_op jit(solution)/shard_map/attention/pallas_call | solution.py:774
  85.2 102.3 %feed_forward.1 = (bf16[512,768]{1,0:T(8,128)(2,1)}, f32[512,768]{1,0:T(8,128)}, f32[24,768]{1,0:T(8,128)}, f32[24,768]{1,0:T(8,128)}, f32[24,3072]{1,0:T(8,128)...) custom-call(bf16[512,768]{1,0:T(8,128)(2,1)} %bitcast.17, bf16[512,768]{1,0:T(8,128)(2,1)} %bitcast.19, ...), custom_call_target="tpu_custom_call" | custom-call | tf_op jit(solution)/shard_map/feed_forward/pallas_call | solution.py:1148
  187.5 3.6 %place.1 = (bf16[512,768]{1,0:T(8,128)(2,1)}, f32[512,768]{1,0:T(8,128)}, f32[24,768]{1,0:T(8,128)}, f32[24,128]{1,0:T(8,128)}, f32[24,768]{1,0:T(8,128)}, /*ind...) custom-call(f32[16,768]{1,0:T(8,128)} %get-tuple-element.52.small, ...), custom_call_target="tpu_custom_call" | custom-call | tf_op jit(solution)/shard_map/place/pallas_call | solution.py:1199
where the time goes:
time: 191 us
  Pallas kernels  190 us (99%)
    pallas_call x1, Pallas kernels, feed_forward(): pl.pallas_call(feed_kernel, out_shape=(out((rows, 768), b16), out((rows,...  102 us
    pallas_call x1, Pallas kernels, attention_call(): pl.pallas_call(attention_kernel, out_shape=(out((32,) + w_up.shape, b16),...  84.6 us

commit v1 on v0

--- a/solution.py
+++ b/solution.py
@@ -293,7 +293,7 @@
 NT = (((1,), (1,)), ((), ()))
 VM = pl.BlockSpec(memory_space=pltpu.VMEM)
 HBM = pl.BlockSpec(memory_space=pl.ANY)
-GROUP = 4
+GROUP = 6
 KEYS = 512
 MINI = 256
 scale_log2 = 0.125 * 1.4426950408889634
@@ -694,23 +694,17 @@
         return act
 
     actions = [
-        lambda: gather_d.from_z(1),
-        lambda: gather_d.from_xy(0),
+        then(lambda: gather_d.from_z(1), lambda: gather_d.from_xy(0)),
         None,
         then(each("from_z", 2), lambda: gather_u.from_diagonal(0)),
         each("from_xy", 1),
-        lambda: gather_d.from_diagonal(0),
-        each("from_z", 3),
+        then(lambda: gather_d.from_diagonal(0), each("from_z", 3)),
         each("from_diagonal", 1),
         each("from_xy", 2),
-        None,
         each("from_diagonal", 2),
-        None,
         each("from_xy", 3),
         None,
-        None,
         each("from_diagonal", 3),
-        None,
         None,
     ]
 

time: 191 us -> 189 us (0.990)
    pallas_call x1, Pallas kernels: 102 us -> 100 us  [feed_forward(): pl.pallas_call(feed_kernel, out_shape=(out((rows, 768), b16), out((rows,...]
where the time goes in v1:
time: 189 us
  Pallas kernels  189 us (100%)
    pallas_call x1, Pallas kernels, feed_forward(): pl.pallas_call(feed_kernel, out_shape=(out((rows, 768), b16), out((rows,...  100 us
    pallas_call x1, Pallas kernels, attention_call(): pl.pallas_call(attention_kernel, out_shape=(out((32,) + w_up.shape, b16),...  84.6 us

profile of v1, /device:TPU:0, one launch (start us, length us, event | category | flops | bytes accessed | tf_op | source)
XLA Modules:
  0.0 189.3 jit_solution(11242303050539591555)
XLA Ops:
  0.6 84.6 %attention.1 = (bf16[32,24,3072]{2,1,0:T(8,128)(2,1)}, bf16[32,96,768]{2,1,0:T(8,128)(2,1)}, f32[8,768]{1,0:T(8,128)}, f32[1,3072]{1,0:T(1,128)}, bf16[768,128]{...) custom-call(bf16[512,768]{1,0:T(8,128)(2,1)} %bitcast.16, ...), custom_call_target="tpu_custom_call" | custom-call | tf_op jit(solution)/shard_map/attention/pallas_call | solution.py:768
  85.3 100.2 %feed_forward.1 = (bf16[512,768]{1,0:T(8,128)(2,1)}, f32[512,768]{1,0:T(8,128)}, f32[24,768]{1,0:T(8,128)}, f32[24,768]{1,0:T(8,128)}, f32[24,3072]{1,0:T(8,128)...) custom-call(bf16[512,768]{1,0:T(8,128)(2,1)} %bitcast.17, bf16[512,768]{1,0:T(8,128)(2,1)} %bitcast.19, ...), custom_call_target="tpu_custom_call" | custom-call | tf_op jit(solution)/shard_map/feed_forward/pallas_call | solution.py:1142
  185.6 3.6 %place.1 = (bf16[512,768]{1,0:T(8,128)(2,1)}, f32[512,768]{1,0:T(8,128)}, f32[24,768]{1,0:T(8,128)}, f32[24,128]{1,0:T(8,128)}, f32[24,768]{1,0:T(8,128)}, /*ind...) custom-call(f32[16,768]{1,0:T(8,128)} %get-tuple-element.52.small, ...), custom_call_target="tpu_custom_call" | custom-call | tf_op jit(solution)/shard_map/place/pallas_call | solution.py:1193

commit v2 on v1

--- a/solution.py
+++ b/solution.py
@@ -1015,8 +1015,8 @@
     chunk(3, True)
     scatter_d.diagonal()
     chunk(1, False)
+    scatter_d.beside(1)
     scatter_a.own()
-    scatter_d.beside(1)
     for flip in (1, 2, 3):
         kv_arrived(flip, dkv_z.at[flip - 1])
     cosine, sine_part = cos_ref[...], sin_ref[...]

time: 189 us -> 190 us (level)
  no operation moved by 1% of the time
where the time goes in v2:
time: 190 us
  Pallas kernels  189 us (99%)
    pallas_call x1, Pallas kernels, feed_forward(): pl.pallas_call(feed_kernel, out_shape=(out((rows, 768), b16), out((rows,...  101 us
    pallas_call x1, Pallas kernels, attention_call(): pl.pallas_call(attention_kernel, out_shape=(out((32,) + w_up.shape, b16),...  84.6 us

profile of v2, /device:TPU:0, one launch (start us, length us, event | category | flops | bytes accessed | tf_op | source)
XLA Modules:
  0.0 189.7 jit_solution(7542717254273013949)
XLA Ops:
  0.6 84.6 %attention.1 = (bf16[32,24,3072]{2,1,0:T(8,128)(2,1)}, bf16[32,96,768]{2,1,0:T(8,128)(2,1)}, f32[8,768]{1,0:T(8,128)}, f32[1,3072]{1,0:T(1,128)}, bf16[768,128]{...) custom-call(bf16[512,768]{1,0:T(8,128)(2,1)} %bitcast.16, ...), custom_call_target="tpu_custom_call" | custom-call | tf_op jit(solution)/shard_map/attention/pallas_call | solution.py:768
  85.3 100.6 %feed_forward.1 = (bf16[512,768]{1,0:T(8,128)(2,1)}, f32[512,768]{1,0:T(8,128)}, f32[24,768]{1,0:T(8,128)}, f32[24,768]{1,0:T(8,128)}, f32[24,3072]{1,0:T(8,128)...) custom-call(bf16[512,768]{1,0:T(8,128)(2,1)} %bitcast.17, bf16[512,768]{1,0:T(8,128)(2,1)} %bitcast.19, ...), custom_call_target="tpu_custom_call" | custom-call | tf_op jit(solution)/shard_map/feed_forward/pallas_call | solution.py:1142
  185.9 3.6 %place.1 = (bf16[512,768]{1,0:T(8,128)(2,1)}, f32[512,768]{1,0:T(8,128)}, f32[24,768]{1,0:T(8,128)}, f32[24,128]{1,0:T(8,128)}, f32[24,768]{1,0:T(8,128)}, /*ind...) custom-call(f32[16,768]{1,0:T(8,128)} %get-tuple-element.52.small, ...), custom_call_target="tpu_custom_call" | custom-call | tf_op jit(solution)/shard_map/place/pallas_call | solution.py:1193
